TPU v7x, 32 devices: a whole 2x2x4 slice. The times are simulated.
32 devices in a mesh: dp: 8 (over z, x), tensor: 4 (over y, core).
Axes of the slice: x: 2, y: 2, z: 4, core: 2. Of those that a mesh axis runs over, the one named last changes fastest.
Arguments:
- tokens: bfloat16 [24576, 1024], P('dp'), may hold values from -6 to 6
- starts: int32 [24576], P('dp'), may hold values from 0 to 1, as said below
- norm_gains: float32 [2, 1024], replicated, may hold values from 0.1 to 1.9
- in_weight: bfloat16 [3, 1024, 1024], P(None, None, 'tensor'), may hold values from -0.1875 to 0.1875
- conv_weight: float32 [3, 1024], P(None, 'tensor'), may hold values from -3 to 3
- out_weight: bfloat16 [1024, 1024], P('tensor'), may hold values from -0.1875 to 0.1875
- ffn_weight: bfloat16 [2, 1024, 4608], P(None, None, 'tensor'), may hold values from -0.1875 to 0.1875
- down_weight: bfloat16 [4608, 1024], P('tensor'), may hold values from -0.1875 to 0.1875
- cotangent: bfloat16 [24576, 1024], P('dp'), may hold values from -6 to 6
Outputs:
- block_out: bfloat16 [24576, 1024], P(('dp', 'tensor'))
- grad_tokens: float32 [24576, 1024], P(('dp', 'tensor'))
- grad_gains: float32 [2, 1024], replicated
- grad_in_weight: float32 [3, 1024, 1024], P(None, 'dp', 'tensor')
- grad_conv: float32 [3, 1024], replicated
- grad_out_weight: float32 [1024, 1024], P('tensor', 'dp')
- grad_ffn: float32 [2, 1024, 4608], P(None, 'dp', 'tensor')
- grad_down: float32 [4608, 1024], P('tensor', 'dp')
Inputs may be any that keep to these rules, and one draw needn't show every extreme that they name: starts[0], starts[3071] and starts[21505] are 1, and starts is 0 at every token between the last two, so one document runs from token 3071 to token 21504; further documents may begin anywhere among the first 3071 tokens and the last 3070.
All inputs are finite; a program needn't handle non-finite values.
Results may differ from a plain program's by a relative error of at most 0.024.
Values may be sent and summed in bfloat16 or wider, within the bound.
No kernel may reach another device: no remote copies, remote signals or barrier semaphores. Data moves between devices by JAX's collectives and lax.ppermute only.
A program may use at most 256 MiB of HBM per device.

v0:
```python
import jax
import jax.numpy as jnp
from jax import lax
from jax.sharding import PartitionSpec as P

EPSILON = 1e-05


def from_behind(value, axis, by):
    peers = lax.axis_size(axis)
    pairs = [(i, i + by) for i in range(peers) if 0 <= i + by < peers]
    return lax.ppermute(value, axis, pairs)


def inverse_rms(values):
    return lax.rsqrt(jnp.mean(values * values, axis=-1, keepdims=True) + EPSILON)


def norm_backward(grad_normed, normed, inverse, gain):
    scaled = grad_normed * gain
    return inverse * (scaled - normed * jnp.mean(scaled * normed, axis=-1, keepdims=True))


def body(
    tokens,
    starts,
    norm_gains,
    in_weight,
    conv_weight,
    out_weight,
    ffn_weight,
    down_weight,
    cotangent,
):
    row_count = tokens.shape[0]
    channels = in_weight.shape[2]
    tensor_count = lax.axis_size("tensor")
    share_rows = row_count // tensor_count
    first_row = lax.axis_index("tensor") * share_rows
    x_full = tokens.astype(jnp.float32)
    keep_mask = 1.0 - starts.astype(jnp.float32)
    inverse_one = inverse_rms(x_full)
    x_normed = x_full * inverse_one
    normed_in = (x_normed * norm_gains[0]).astype(jnp.bfloat16)
    projected = jnp.einsum("td,kdc->ktc", normed_in, in_weight, preferred_element_type=jnp.float32)
    mixed_low = (projected[0] * projected[2]).astype(jnp.bfloat16)
    edge_rows = jnp.stack(
        [mixed_low[-1], (mixed_low[-2].astype(jnp.float32) * keep_mask[-1]).astype(jnp.bfloat16)]
    )
    received = from_behind(edge_rows, "dp", 1).astype(jnp.float32)
    mixed_full = mixed_low.astype(jnp.float32)
    prev_one = jnp.concatenate([received[0:1], mixed_full[:-1]], 0)
    prev_two = jnp.concatenate(
        [
            received[1:2],
            keep_mask[:-1, None] * jnp.concatenate([received[0:1], mixed_full[:-2]], 0),
        ],
        0,
    )
    conv_out = conv_weight[2] * mixed_full + keep_mask[:, None] * (
        conv_weight[1] * prev_one + conv_weight[0] * prev_two
    )
    gated_mix = (projected[1] * conv_out).astype(jnp.bfloat16)
    resid = x_full + lax.psum(
        jnp.dot(gated_mix, out_weight, preferred_element_type=jnp.float32).astype(jnp.bfloat16),
        "tensor",
    ).astype(jnp.float32)
    inverse_two = inverse_rms(resid)
    resid_normed = resid * inverse_two
    normed_ffn = (resid_normed * norm_gains[1]).astype(jnp.bfloat16)
    resid_share = lax.dynamic_slice_in_dim(resid, first_row, share_rows, 0)
    gate_up = jnp.einsum("td,kdf->ktf", normed_ffn, ffn_weight, preferred_element_type=jnp.float32)
    sigmoid_gate = jax.nn.sigmoid(gate_up[0])
    silu_gate = gate_up[0] * sigmoid_gate
    activation = (silu_gate * gate_up[1]).astype(jnp.bfloat16)
    block_out = (
        resid_share
        + lax.psum_scatter(
            jnp.dot(activation, down_weight, preferred_element_type=jnp.float32).astype(
                jnp.bfloat16
            ),
            "tensor",
            scatter_dimension=0,
            tiled=True,
        ).astype(jnp.float32)
    ).astype(jnp.bfloat16)
    grad_down = jnp.einsum("tf,td->fd", activation, cotangent, preferred_element_type=jnp.float32)
    d_act = jnp.einsum("td,fd->tf", cotangent, down_weight, preferred_element_type=jnp.float32)
    d_gate = d_act * gate_up[1] * sigmoid_gate * (1.0 + gate_up[0] * (1.0 - sigmoid_gate))
    d_gate_up = jnp.stack([d_gate, d_act * silu_gate]).astype(jnp.bfloat16)
    grad_ffn = jnp.einsum("ktf,td->kdf", d_gate_up, normed_ffn, preferred_element_type=jnp.float32)
    d_nf = lax.psum(
        jnp.einsum("ktf,kdf->td", d_gate_up, ffn_weight, preferred_element_type=jnp.float32).astype(
            jnp.bfloat16
        ),
        "tensor",
    ).astype(jnp.float32)
    d_res = cotangent.astype(jnp.float32) + norm_backward(
        d_nf, resid_normed, inverse_two, norm_gains[1]
    )
    d_res_low = d_res.astype(jnp.bfloat16)
    d_res_share = lax.dynamic_slice_in_dim(d_res, first_row, share_rows, 0)
    gain_two = jnp.sum(
        lax.dynamic_slice_in_dim(d_nf, first_row, share_rows, 0)
        * lax.dynamic_slice_in_dim(resid_normed, first_row, share_rows, 0),
        axis=0,
    )
    grad_out = jnp.einsum("tc,td->cd", gated_mix, d_res_low, preferred_element_type=jnp.float32)
    d_gated = jnp.einsum("td,cd->tc", d_res_low, out_weight, preferred_element_type=jnp.float32)
    d_cgate = d_gated * conv_out
    d_conv = d_gated * projected[1]
    weighted = keep_mask[:, None] * d_conv
    edge_back = jnp.stack(
        [
            conv_weight[1] * weighted[0] + conv_weight[0] * keep_mask[0] * weighted[1],
            conv_weight[0] * weighted[0],
        ]
    )
    after = from_behind(edge_back, "dp", -1)
    next_one = jnp.concatenate([weighted[1:], jnp.zeros((1, channels), jnp.float32)], 0)
    next_two = jnp.concatenate([weighted[2:], jnp.zeros((2, channels), jnp.float32)], 0)
    keep_next = jnp.concatenate([keep_mask[1:], jnp.ones((1,), jnp.float32)])
    tail_rows = jnp.concatenate(
        [
            jnp.zeros((row_count - 2, channels), jnp.float32),
            jnp.stack([keep_mask[-1] * after[1], after[0]]),
        ],
        0,
    )
    d_mixed = (
        conv_weight[2] * d_conv
        + conv_weight[1] * next_one
        + conv_weight[0] * keep_next[:, None] * next_two
        + tail_rows
    )
    conv_local = jnp.stack(
        [
            jnp.sum(weighted * prev_two, axis=0),
            jnp.sum(weighted * prev_one, axis=0),
            jnp.sum(d_conv * mixed_full, axis=0),
        ]
    )
    d_proj = jnp.stack([d_mixed * projected[2], d_cgate, d_mixed * projected[0]]).astype(
        jnp.bfloat16
    )
    grad_in = jnp.einsum("ktc,td->kdc", d_proj, normed_in, preferred_element_type=jnp.float32)
    d_ni = lax.psum_scatter(
        jnp.einsum("ktc,kdc->td", d_proj, in_weight, preferred_element_type=jnp.float32).astype(
            jnp.bfloat16
        ),
        "tensor",
        scatter_dimension=0,
        tiled=True,
    ).astype(jnp.float32)
    x_normed_share = lax.dynamic_slice_in_dim(x_normed, first_row, share_rows, 0)
    inverse_share = lax.dynamic_slice_in_dim(inverse_one, first_row, share_rows, 0)
    grad_tokens = d_res_share + norm_backward(d_ni, x_normed_share, inverse_share, norm_gains[0])
    gain_one = jnp.sum(d_ni * x_normed_share, axis=0)
    conv_full = lax.dynamic_update_slice(
        jnp.zeros((3, channels * tensor_count), jnp.float32),
        conv_local,
        (0, lax.axis_index("tensor") * channels),
    )
    grad_gains, grad_conv = lax.psum((jnp.stack([gain_one, gain_two]), conv_full), ("dp", "tensor"))
    summed = (
        lax.psum_scatter(
            grad_in.astype(jnp.bfloat16), "dp", scatter_dimension=1, tiled=True
        ).astype(jnp.float32),
        lax.psum_scatter(
            grad_out.astype(jnp.bfloat16), "dp", scatter_dimension=1, tiled=True
        ).astype(jnp.float32),
        lax.psum_scatter(
            grad_ffn.astype(jnp.bfloat16), "dp", scatter_dimension=1, tiled=True
        ).astype(jnp.float32),
        lax.psum_scatter(
            grad_down.astype(jnp.bfloat16), "dp", scatter_dimension=1, tiled=True
        ).astype(jnp.float32),
    )
    return (
        block_out,
        grad_tokens,
        grad_gains,
        summed[0],
        grad_conv,
        summed[1],
        summed[2],
        summed[3],
    )


def solution(mesh):
    return jax.shard_map(
        body,
        mesh=mesh,
        in_specs=(
            P("dp", None),
            P("dp"),
            P(),
            P(None, None, "tensor"),
            P(None, "tensor"),
            P("tensor", None),
            P(None, None, "tensor"),
            P("tensor", None),
            P("dp", None),
        ),
        out_specs=(
            P(("dp", "tensor"), None),
            P(("dp", "tensor"), None),
            P(),
            P(None, "dp", "tensor"),
            P(),
            P("tensor", "dp"),
            P(None, "dp", "tensor"),
            P("tensor", "dp"),
        ),
        check_vma=False,
    )
```

profile of v0, /device:TPU:0, one launch (start us, length us, event | category | flops | bytes accessed | tf_op | source)
XLA Modules:
  0.0 873.9 jit_solution(3791946883630916368)
XLA Ops:
  12.6 6.8 convolution_bitcast_fusion.1
  37.7 121.5 %all-reduce.6.cloned.1.call-done = bf16[3072,1024]{1,0:T(8,128)(2,1)} async-done(((bf16[3072,1024]{1,0:T(8,128)(2,1)}), bf16[3072,1024]{1,0:T(8,128)(2,1)}) %all-reduce.6.cloned.1.call-update) | async-done | bytes 6291472 | tf_op jit(solution)/shard_map/psum | solution.py:64
  159.2 11.3 %convert_add_fusion = (f32[3072,1024]{1,0:T(8,128)}, f32[3072]{0:T(1024)S(1)}) fusion(bf16[3072,1024]{1,0:T(8,128)(2,1)} %param.9, bf16[3072,1024]{1,0:T(8,128)(2,1)} %all-reduce.6.cloned.1.call-done), kind=kLoop, calls=%fused_computation.1 | loop fusion | flops 15725568 | bytes 25178112 | tf_op jit(solution)/shard_map/add | solution.py:64
  170.5 11.4 %convert_multiply_fusion = (f32[3072,1024]{1,0:T(8,128)}, f32[3072,1024]{1,0:T(8,128)S(1)}) fusion(bf16[3072,1024]{1,0:T(8,128)(2,1)} %param.9, f32[3072]{0:T(1024)S(1)} %add_rsqrt_fusion.1, f32[3072]{0:T(1024)S(1)} %add_rsqrt_fusion, bf16[3072,1024]{1,0:T(8,128)(2,1)} %all-reduce.6.cloned.1.call-done), kind=kLoop, calls=%fused_computation.2 | loop fusion | flops 15728640 | bytes 37773312 | tf_op jit(solution)/shard_map/mul | solution.py:43
  186.3 18.2 %convolution_bitcast_fusion = f32[2,3072,1152]{2,1,0:T(8,128)} fusion(bf16[2,1024,1152]{2,1,0:T(8,128)(2,1)S(1)} %bitcast.147, f32[3072,1024]{1,0:T(8,128)S(1)} %get-tuple-element.25, f32[1024]{0:T(1024)S(1)} %bitcast.128), kind=kOutput, calls=%fused_computation | convolution fusion | flops 14501806080 | bytes 45617152 | tf_op jit(solution)/shard_map/td,kdf->ktf/dot_general | solution.py:72
  204.6 25.4 %fusion.5 = (bf16[1,3072,1152]{2,1,0:T(8,128)(2,1)}, bf16[1,3072,1152]{2,1,0:T(8,128)(2,1)}, bf16[3072,1152]{1,0:T(8,128)(2,1)}) fusion(f32[2,3072,1152]{2,1,0:T(8,128)} %convolution_bitcast_fusion, bf16[3072,1024]{1,0:T(8,128)(2,1)} %param.17, bf16[1152,1024]{1,0:T(8,128)(2,1)S(1)} %copy-done), kind=kOutput, calls=%fused_computation.23 | convolution fusion | flops 7300841472 | bytes 58195968 | tf_op jit(solution)/shard_map/td,fd->tf/dot_general | solution.py:88
  230.0 20.8 %bitcast_convert_fusion.1 = bf16[3072,1024]{1,0:T(8,128)(2,1)} fusion(bf16[2,1024,1152]{2,1,0:T(8,128)(2,1)} %param.15, bf16[1,3072,1152]{2,1,0:T(8,128)(2,1)} %get-tuple-element.18, bf16[1,3072,1152]{2,1,0:T(8,128)(2,1)} %get-tuple-element.17), kind=kOutput, calls=%fused_computation.14 | convolution fusion | flops 14505738240 | bytes 25165824 | tf_op jit(solution)/shard_map/ktf,kdf->td/dot_general | solution.py:93
  250.9 119.9 %all-reduce.8.cloned.1.call-done = bf16[3072,1024]{1,0:T(8,128)(2,1)} async-done(((bf16[3072,1024]{1,0:T(8,128)(2,1)}), bf16[3072,1024]{1,0:T(8,128)(2,1)}) %all-reduce.8.cloned.1.call-update) | async-done | bytes 6291472 | tf_op jit(solution)/shard_map/psum | solution.py:92
  370.8 8.1 multiply_reduce_fusion
  378.9 9.6 %multiply_add_fusion = f32[3072,1024]{1,0:T(8,128)S(1)} fusion(f32[3072,1024]{1,0:T(8,128)} %copy-done.2, bf16[3072,1024]{1,0:T(8,128)(2,1)} %param.17, f32[3072]{0:T(1024)S(1)} %broadcast_multiply_fusion.2, bf16[3072,1024]{1,0:T(8,128)(2,1)} %all-reduce.8.cloned.1.call-done, f32[1024]{0:T(1024)S(1)} %bitcast.130, f32[3072]{0:T(1024)S(1)} %add_rsqrt_fusion), kind=kLoop, calls=%fused_computation.15 | loop fusion | flops 22020096 | bytes 37777408 | tf_op jit(solution)/shard_map/add | solution.py:98
  396.0 12.7 %convolution_convert_fusion.2 = bf16[1152,1024]{1,0:T(8,128)(2,1)} fusion(bf16[3072,1152]{1,0:T(8,128)(2,1)} %get-tuple-element.19, bf16[3072,1024]{1,0:T(8,128)(2,1)} %param.17), kind=kOutput, calls=%fused_computation.35 | convolution fusion | flops 7248936960 | bytes 15728640 | tf_op jit(solution)/shard_map/tf,td->fd/dot_general | solution.py:87
  420.3 7.6 multiply_reduce_fusion.4
  436.5 9.2 %concatenate.27 = f32[3072,256]{1,0:T(8,128)} concatenate(f32[3070,256]{1,0:T(8,128)} %broadcast_in_dim.4, f32[1,256]{1,0:T(1,128)S(1)} %get-tuple-element.38, f32[1,256]{1,0:T(1,128)S(1)} %get-tuple-element.37), dimensions={0} | concatenate | bytes 6291456 | tf_op jit(solution)/shard_map/concatenate | solution.py:123
  445.7 7.4 fusion.23
  457.2 9.7 %fusion.26 = bf16[3,1024,256]{2,1,0:T(8,128)(2,1)} fusion(bf16[1,3072,256]{2,1,0:T(8,128)(2,1)S(1)} %fusion.25, bf16[1,3072,256]{2,1,0:T(8,128)(2,1)S(1)} %copy-done.14, bf16[1,3072,256]{2,1,0:T(8,128)(2,1)S(1)} %get-tuple-element.15, f32[1024]{0:T(1024)S(1)} %bitcast.125, bf16[3072,1024]{1,0:T(8,128)(2,1)} %param.9, f32[3072]{0:T(1024)S(1)} %copy-done.20), kind=kOutput, calls=%fused_computation.71 | convolution fusion | flops 4859363328 | bytes 12599296 | tf_op jit(solution)/shard_map/ktc,td->kdc/dot_general | solution.py:146
  467.2 23.1 %fusion.9 = bf16[2,1024,1152]{2,1,0:T(8,128)(2,1)} fusion(bf16[1,3072,1152]{2,1,0:T(8,128)(2,1)} %get-tuple-element.18, bf16[1,3072,1152]{2,1,0:T(8,128)(2,1)} %get-tuple-element.17, f32[3072,1024]{1,0:T(8,128)} %copy-done.2, f32[1024]{0:T(1024)S(1)} %bitcast.131), kind=kOutput, calls=%fused_computation.32 | convolution fusion | flops 14532476928 | bytes 31461376 | tf_op jit(solution)/shard_map/ktf,td->kdf/dot_general | solution.py:91
  490.3 13.3 %convolution_convert_fusion.1 = bf16[3072,1024]{1,0:T(8,128)(2,1)} fusion(bf16[3072,1152]{1,0:T(8,128)(2,1)} %get-tuple-element.19, bf16[1152,1024]{1,0:T(8,128)(2,1)S(1)} %copy-done), kind=kOutput, calls=%fused_computation.29 | convolution fusion | flops 7250903040 | bytes 15728640 | tf_op jit(solution)/shard_map/dot_general | solution.py:79
  503.9 9.7 %bitcast_convert_fusion = bf16[3072,1024]{1,0:T(8,128)(2,1)} fusion(bf16[3,1024,256]{2,1,0:T(8,128)(2,1)} %param.12, bf16[1,3072,256]{2,1,0:T(8,128)(2,1)} %copy-done.16, bf16[1,3072,256]{2,1,0:T(8,128)(2,1)} %get-tuple-element.23, bf16[1,3072,256]{2,1,0:T(8,128)(2,1)} %copy-done.15), kind=kOutput, calls=%fused_computation.13 | convolution fusion | flops 4839702528 | bytes 12582912 | tf_op jit(solution)/shard_map/ktc,kdc->td/dot_general | solution.py:148
  522.3 7.7 reduce-scatter.21.cloned.1.call-done
  532.0 66.3 %reduce-scatter.15.cloned.1.call-done = bf16[3,128,256]{2,1,0:T(8,128)(2,1)} async-done(((bf16[3,1024,256]{2,1,0:T(8,128)(2,1)}), bf16[3,128,256]{2,1,0:T(8,128)(2,1)}) %reduce-scatter.15.cloned.1.call-update) | async-done | bytes 196624 | tf_op jit(solution)/shard_map/reduce_scatter | solution.py:166
  600.0 96.1 %reduce-scatter.17.cloned.1.call-done = bf16[2,128,1152]{2,1,0:T(8,128)(2,1)} async-done(((bf16[2,1024,1152]{2,1,0:T(8,128)(2,1)}), bf16[2,128,1152]{2,1,0:T(8,128)(2,1)}) %reduce-scatter.17.cloned.1.call-update) | async-done | bytes 589840 | tf_op jit(solution)/shard_map/reduce_scatter | solution.py:172
  698.2 58.5 %reduce-scatter.11.cloned.1.call-done = bf16[768,1024]{1,0:T(8,128)(2,1)} async-done(((bf16[3072,1024]{1,0:T(8,128)(2,1)}), bf16[768,1024]{1,0:T(8,128)(2,1)}) %reduce-scatter.11.cloned.1.call-update) | async-done | bytes 1572880 | tf_op jit(solution)/shard_map/reduce_scatter | solution.py:78
  760.8 57.0 %reduce-scatter.13.cloned.1.call-done = bf16[768,1024]{1,0:T(8,128)(2,1)} async-done(((bf16[3072,1024]{1,0:T(8,128)(2,1)}), bf16[768,1024]{1,0:T(8,128)(2,1)}) %reduce-scatter.13.cloned.1.call-update) | async-done | bytes 1572880 | tf_op jit(solution)/shard_map/reduce_scatter | solution.py:147
  821.0 39.9 %all-reduce.2 = (f32[2,1024]{1,0:T(2,128)}, f32[3,1024]{1,0:T(4,128)}) all-reduce(f32[2,1024]{1,0:T(2,128)S(1)} %pad_maximum_fusion.19, f32[3,1024]{1,0:T(4,128)S(1)} %maximum_dynamic-update-slice_fusion), channel_id=1, replica_groups=mesh['dp'=8,'tensor'=4] {'dp','tensor'}, use_global_device_ids=true, to_apply=%region_10.0 | all-reduce | flops 5120 | bytes 40960 | tf_op jit(solution)/shard_map/psum | solution.py:164
  (147 shorter events, 87.6 us)
Async XLA Ops:
  7.2 197.4 %copy-start = (bf16[1152,1024]{1,0:T(8,128)(2,1)S(1)}, bf16[1152,1024]{1,0:T(8,128)(2,1)}, u32[]{:S(2)}) copy-start(bf16[1152,1024]{1,0:T(8,128)(2,1)} %param.16) | copy-start | bytes 7077892
  7.2 152.0 %all-reduce.6.cloned.1.call-start = ((), (), s32[]{:S(2)}) async-start(), calls=%async_computation.6 | async-start | bytes 12582912 | tf_op jit(solution)/shard_map/psum | solution.py:64
  8.1 11.3 %copy-start.22 = (f32[1,1024]{1,0:T(1,128)}, f32[1,1024]{1,0:T(1,128)S(1)}, u32[]{:S(2)}) copy-start(f32[1,1024]{1,0:T(1,128)S(1)} %get-tuple-element.33) | copy-start | bytes 12292
  12.5 157.9 %copy-start.19 = (f32[3072]{0:T(1024)}, f32[3072]{0:T(1024)S(1)}, u32[]{:S(2)}) copy-start(f32[3072]{0:T(1024)S(1)} %add_rsqrt_fusion.1) | copy-start | bytes 36868
  19.4 10.0 %copy-start.3 = (f32[3,3072,256]{2,1,0:T(8,128)}, f32[3,3072,256]{2,1,0:T(8,128)S(1)}, u32[]{:S(2)}) copy-start(f32[3,3072,256]{2,1,0:T(8,128)S(1)} %convolution_bitcast_fusion.1) | copy-start | bytes 28311556
  19.4 7.8 copy-start.35
  20.2 9.3 %copy-start.17 = (f32[3072]{0:T(1024)}, f32[3072]{0:T(1024)S(1)}, u32[]{:S(2)}) copy-start(f32[3072]{0:T(1024)S(1)} %convert_subtract_fusion) | copy-start | bytes 36868
  21.8 6.1 collective-permute-start
  37.4 333.4 %all-reduce.8.cloned.1.call-start = ((), (), s32[]{:S(2)}) async-start(), calls=%async_computation.8 | async-start | bytes 12582912 | tf_op jit(solution)/shard_map/psum | solution.py:92
  159.2 27.2 %slice-start = ((s8[4718592]{0:T(1024)(128)(4,1)}), s8[524288]{0:T(1024)(128)(4,1)S(1)}, s32[]{:S(2)}) async-start(s8[4718592]{0:T(1024)(128)(4,1)} %bitcast.146), calls=%async_computation.14 | async-start | bytes 1048576
  170.5 15.9 %slice-start.1 = ((s8[4718592]{0:T(1024)(128)(4,1)}), s8[4194304]{0:T(1024)(128)(4,1)S(1)}, s32[]{:S(2)}) async-start(s8[4718592]{0:T(1024)(128)(4,1)} %bitcast.146), calls=%async_computation.15 | async-start | bytes 8388608
  250.8 269.8 %reduce-scatter.19.cloned.1.call-start = ((), (), s32[]{:S(2)}) async-start(), calls=%async_computation.12 | async-start | bytes 589824
  378.9 14.2 %copy-start.11 = (bf16[3072,256]{1,0:T(8,128)(2,1)S(1)}, bf16[3072,256]{1,0:T(8,128)(2,1)}, u32[]{:S(2)}) copy-start(bf16[3072,256]{1,0:T(8,128)(2,1)} %copy-done.10) | copy-start | bytes 4718596
  395.9 134.0 %reduce-scatter.21.cloned.1.call-start = ((), (), s32[]{:S(2)}) async-start(), calls=%async_computation.13 | async-start | bytes 2654208
  413.1 7.1 copy-start.18
  413.1 7.1 copy-start.25
  413.2 185.1 %reduce-scatter.15.cloned.1.call-start = ((), (), s32[]{:S(2)}) async-start(), calls=%async_computation.10 | async-start | bytes 1769472 | tf_op jit(solution)/shard_map/reduce_scatter | solution.py:166
  420.3 7.6 copy-start.5
  420.3 7.6 copy-start.36
  420.3 9.6 %copy-start.21 = (f32[3071]{0:T(1024)S(1)}, f32[3071]{0:T(1024)}, u32[]{:S(2)}) copy-start(f32[3071]{0:T(1024)} %get-tuple-element.28) | copy-start | bytes 36856
  428.6 5.5 collective-permute-start.1
  466.9 229.1 %reduce-scatter.17.cloned.1.call-start = ((), (), s32[]{:S(2)}) async-start(), calls=%async_computation.11 | async-start | bytes 5308416 | tf_op jit(solution)/shard_map/reduce_scatter | solution.py:172
  490.3 266.5 %reduce-scatter.11.cloned.1.call-start = ((), (), s32[]{:S(2)}) async-start(), calls=%async_computation.7 | async-start | bytes 7864320 | tf_op jit(solution)/shard_map/reduce_scatter | solution.py:78
  503.6 314.2 %reduce-scatter.13.cloned.1.call-start = ((), (), s32[]{:S(2)}) async-start(), calls=%async_computation.9 | async-start | bytes 7864320 | tf_op jit(solution)/shard_map/reduce_scatter | solution.py:147
  (25 other events, 103.6 us)
Sparse Core Ops, SparseCore 0:
  37.5 121.6 all-reduce.5
  251.0 119.7 all-reduce.7
  396.0 62.0 reduce-scatter.18
  461.9 68.0 reduce-scatter.20
  533.7 64.5 reduce-scatter.14
  601.8 94.2 reduce-scatter.16
  698.6 58.1 reduce-scatter.10
  759.4 58.3 reduce-scatter.12
where the time goes:
time: 883 us; the launch traced here: 874 us
  waiting for transfers between devices  527 us (60%)
  matrix products  153 us (17%)
  other arithmetic  93.9 us (11%)
  blocking collectives  39.9 us (5%)
  local copies, waits for them, and re-layouts  37.3 us (4%)
  between operations  15.2 us (2%)
    psum x1, waiting for transfers between devices, body(): lax.psum(jnp.dot(gated_mix, out_weight, preferred_element_type=jnp.float3...  122 us
    psum x1, waiting for transfers between devices, body(): lax.psum(jnp.einsum('ktf,kdf->td', d_gate_up, ffn_weight, preferred_eleme...  120 us
    reduce_scatter x1, waiting for transfers between devices, body(): lax.psum_scatter(grad_ffn.astype(jnp.bfloat16), 'dp', scatter_dimension=1...  96.1 us
    reduce_scatter x1, waiting for transfers between devices, body(): lax.psum_scatter(grad_in.astype(jnp.bfloat16), 'dp', scatter_dimension=1,...  66.3 us
    reduce_scatter x1, waiting for transfers between devices, body(): lax.psum_scatter(jnp.dot(activation, down_weight, preferred_element_type=...  58.5 us
    reduce_scatter x1, waiting for transfers between devices, body(): lax.psum_scatter(jnp.einsum('ktc,kdc->td', d_proj, in_weight, preferred_e...  57 us
    psum x1, blocking collectives, body(): lax.psum((jnp.stack([gain_one, gain_two]), conv_full), ('dp', 'tensor'))  39.9 us
    dot_general x1, matrix products, body(): jnp.einsum('td,fd->tf', cotangent, down_weight, preferred_element_type=jn...  25.4 us
  transfers between devices with their start and end apart: 10, of which 9 were waited for; matrix products, arithmetic and copies ran while one was open for 15% of the time, Pallas kernels for 0%

commit v1 on v0

v1 whole, which is shorter than its diff:
```python
import jax
import jax.numpy as jnp
from jax import lax
from jax.sharding import PartitionSpec as P

EPSILON = 1e-05
F32 = jnp.float32
BF16 = jnp.bfloat16


def swap(value, axis, bits):
    peers = lax.axis_size(axis)
    return lax.ppermute(value, axis, [(i, i ^ bits) for i in range(peers)])


def shift(value, axes, by):
    peers = lax.axis_size(axes)
    return lax.ppermute(value, axes, [(i, i + by) for i in range(peers) if 0 <= i + by < peers])


def gather_pieces(value):
    count = lax.axis_size("tensor")
    pieces = [value] + [None] * (count - 1)
    pieces[1] = swap(value, "tensor", 1)
    for k in range(2, count, 2):
        pieces[k] = swap(value, "tensor", k)
        pieces[k + 1] = swap(pieces[k], "tensor", 1)
    return pieces


def add_low(mine, received):
    return (mine.astype(F32) + received.astype(F32)).astype(BF16)


def scatter_pieces(pieces):
    count = len(pieces)
    evens = [
        add_low(pieces[k], swap(pieces[k + 1], "tensor", 1)) for k in range(0, count, 2)
    ]
    total = evens[0].astype(F32)
    for k in range(2, count, 2):
        total = total + swap(evens[k // 2], "tensor", k).astype(F32)
    return total


def scatter_dp(value):
    count = lax.axis_size("dp")
    index = lax.axis_index("dp")
    bits = 1
    while bits < count:
        side = (index // bits) % 2
        pairs = value.reshape((value.shape[0] // 2, 2) + value.shape[1:])
        sent = lax.dynamic_index_in_dim(pairs, 1 - side, 1, keepdims=False)
        kept = lax.dynamic_index_in_dim(pairs, side, 1, keepdims=False)
        received = swap(sent, "dp", bits)
        value = kept.astype(F32) + received.astype(F32)
        bits *= 2
        if bits < count:
            value = value.astype(BF16)
    return value[0]


def sum_all(value):
    for axis in ("tensor", "dp"):
        bits = 1
        while bits < lax.axis_size(axis):
            value = value + swap(value, axis, bits)
            bits *= 2
    return value


def inverse_rms(values):
    return lax.rsqrt(jnp.mean(values * values, axis=-1, keepdims=True) + EPSILON)


def norm_backward(grad_normed, normed, inverse, gain):
    scaled = grad_normed * gain
    return inverse * (scaled - normed * jnp.mean(scaled * normed, axis=-1, keepdims=True))


def matmul(a, b, dims):
    return lax.dot_general(a, b, (dims, ((), ())), preferred_element_type=F32)


def to_owners(value):
    count = lax.axis_size("tensor")
    here = lax.axis_index("tensor")
    channels = value.shape[1] // count
    result = jnp.zeros(value.shape, value.dtype)
    for k in range(count):
        block = value[:, k * channels : (k + 1) * channels]
        result = lax.dynamic_update_slice(result, block, (0, (here ^ k) * channels))
    return result


def from_owners(value):
    count = lax.axis_size("tensor")
    here = lax.axis_index("tensor")
    channels = value.shape[1] // count
    return jnp.concatenate(
        [lax.dynamic_slice_in_dim(value, (here ^ k) * channels, channels, 1) for k in range(count)], 1
    )


HEAD = 16


def body(
    tokens,
    starts,
    norm_gains,
    in_weight,
    conv_weight,
    out_weight,
    ffn_weight,
    down_weight,
    cotangent,
):
    row_count, width = tokens.shape
    count = lax.axis_size("tensor")
    dp_count = lax.axis_size("dp")
    here = lax.axis_index("tensor")
    rows = row_count // count
    first = here * rows

    keep_all = 1.0 - starts.astype(F32)
    edge = jnp.concatenate(
        [tokens[-HEAD:], jnp.broadcast_to(keep_all[-1], (HEAD, width)).astype(BF16)], 0
    )
    before = shift(edge, "dp", 1)
    back = jnp.maximum(first - HEAD, 0)
    head_rows = jnp.where(
        here == 0, before[:HEAD], lax.dynamic_slice_in_dim(tokens, back, HEAD, 0)
    )
    keep_prev = jnp.where(
        here == 0, before[HEAD, 0].astype(F32), lax.dynamic_index_in_dim(keep_all, jnp.maximum(first - 1, 0), 0, False)
    )
    keep = lax.dynamic_slice_in_dim(keep_all, first, rows, 0)
    keep_before = jnp.concatenate([keep_prev[None], keep[:-1]])[:, None]
    keep_after = jnp.concatenate([keep[1:], jnp.ones((1,), F32)])[:, None]
    keep = keep[:, None]

    in_pieces = gather_pieces(in_weight)
    out_pieces = gather_pieces(out_weight)
    conv_pieces = gather_pieces(conv_weight)
    in_full = jnp.concatenate(in_pieces, 2)
    out_full = jnp.concatenate(out_pieces, 0)
    conv = jnp.concatenate(conv_pieces, 1)

    x_share = lax.dynamic_slice_in_dim(tokens, first, rows, 0)
    x_ext = jnp.concatenate([head_rows, x_share], 0).astype(F32)
    inverse_ext = inverse_rms(x_ext)
    normed_ext = x_ext * inverse_ext
    nin_ext = (normed_ext * norm_gains[0]).astype(BF16)
    x = x_ext[HEAD:]
    inverse_one = inverse_ext[HEAD:]
    x_normed = normed_ext[HEAD:]
    normed_in = nin_ext[HEAD:]
    proj_b = matmul(nin_ext, in_full[0], ((1,), (0,)))
    proj_x = matmul(nin_ext, in_full[2], ((1,), (0,)))
    proj_c = matmul(normed_in, in_full[1], ((1,), (0,)))
    mixed_ext = (proj_b * proj_x).astype(BF16).astype(F32)
    mixed = mixed_ext[HEAD:]
    prev_one = mixed_ext[HEAD - 1 : -1]
    prev_two = keep_before * mixed_ext[HEAD - 2 : -2]
    conv_out = conv[2] * mixed + keep * (conv[1] * prev_one + conv[0] * prev_two)
    gated_mix = (proj_c * conv_out).astype(BF16)
    resid = x + matmul(gated_mix, out_full, ((1,), (0,)))
    inverse_two = inverse_rms(resid)
    resid_normed = resid * inverse_two
    normed_ffn = (resid_normed * norm_gains[1]).astype(BF16)

    nf_pieces = gather_pieces(normed_ffn)
    block_pieces = []
    dnf_pieces = []
    grad_gate = grad_up = grad_down = 0.0
    for pair in range(0, count, 2):
        nf = jnp.concatenate(nf_pieces[pair : pair + 2], 0)
        g = jnp.concatenate(
            [
                lax.dynamic_slice_in_dim(cotangent, (here ^ k) * rows, rows, 0)
                for k in (pair, pair + 1)
            ],
            0,
        )
        gate = matmul(nf, ffn_weight[0], ((1,), (0,)))
        up = matmul(nf, ffn_weight[1], ((1,), (0,)))
        sigmoid = jax.nn.sigmoid(gate)
        silu = gate * sigmoid
        act = (silu * up).astype(BF16)
        d_act = matmul(g, down_weight, ((1,), (1,)))
        d_gate = (d_act * up * sigmoid * (1.0 + gate * (1.0 - sigmoid))).astype(BF16)
        d_up = (d_act * silu).astype(BF16)
        block = matmul(act, down_weight, ((1,), (0,))).astype(BF16)
        d_nf = (
            matmul(d_gate, ffn_weight[0], ((1,), (1,)))
            + matmul(d_up, ffn_weight[1], ((1,), (1,)))
        ).astype(BF16)
        block_pieces += [block[:rows], block[rows:]]
        dnf_pieces += [d_nf[:rows], d_nf[rows:]]
        grad_gate = grad_gate + matmul(nf, d_gate, ((0,), (0,)))
        grad_up = grad_up + matmul(nf, d_up, ((0,), (0,)))
        grad_down = grad_down + matmul(g, act, ((0,), (0,)))

    d_nf = scatter_pieces(dnf_pieces)
    split = (dp_count, width // dp_count, -1)
    out_gate, out_up, out_down = [
        scatter_dp(value.astype(BF16).reshape(split)) for value in (grad_gate, grad_up, grad_down)
    ]
    block_out = (resid + scatter_pieces(block_pieces)).astype(BF16)

    g_share = lax.dynamic_slice_in_dim(cotangent, first, rows, 0).astype(F32)
    d_res = g_share + norm_backward(d_nf, resid_normed, inverse_two, norm_gains[1])
    d_res_low = d_res.astype(BF16)
    gain_two = jnp.sum(d_nf * resid_normed, axis=0)
    d_gated = matmul(d_res_low, out_full, ((1,), (1,)))
    grad_out = matmul(d_res_low, gated_mix, ((0,), (0,))).astype(BF16)
    d_cgate = d_gated * conv_out
    d_conv = d_gated * proj_c
    weighted = keep * d_conv
    edge_back = jnp.stack([weighted[0], keep[0] * weighted[1]])
    after = from_owners(shift(to_owners(edge_back), ("dp", "tensor"), -1))
    next_one = jnp.concatenate([weighted[1:], after[0:1]], 0)
    next_two = jnp.concatenate(
        [keep_after[:-2] * weighted[2:], keep_after[-2:-1] * after[0:1], after[1:2]], 0
    )
    d_mixed = conv[2] * d_conv + conv[1] * next_one + conv[0] * next_two
    conv_local = jnp.stack(
        [
            jnp.sum(weighted * prev_two, axis=0),
            jnp.sum(weighted * prev_one, axis=0),
            jnp.sum(d_conv * mixed, axis=0),
        ]
    )
    d_proj = [
        (d_mixed * proj_x[HEAD:]).astype(BF16),
        d_cgate.astype(BF16),
        (d_mixed * proj_b[HEAD:]).astype(BF16),
    ]
    d_ni = sum(matmul(d_proj[k], in_full[k], ((1,), (1,))) for k in range(3))
    grad_in = [matmul(normed_in, d_proj[k], ((0,), (0,))).astype(BF16) for k in range(3)]
    grad_tokens = d_res + norm_backward(d_ni, x_normed, inverse_one, norm_gains[0])
    gain_one = jnp.sum(d_ni * x_normed, axis=0)

    mixer = jnp.stack(grad_in + [grad_out])
    channels = width // count
    mixer = [
        mixer[:, :, k * channels : (k + 1) * channels].reshape(4, dp_count, width // dp_count, channels).swapaxes(0, 1)
        for k in range(count)
    ]
    mixer = scatter_dp(scatter_pieces(mixer).astype(BF16))

    conv_order = to_owners(conv_local)
    small = sum_all(jnp.concatenate([jnp.stack([gain_one, gain_two]), conv_order], 0))
    return (
        block_out,
        grad_tokens,
        small[:2],
        mixer[:3],
        small[2:],
        mixer[3].T,
        jnp.stack([out_gate, out_up]),
        out_down.T,
    )


def solution(mesh):
    return jax.shard_map(
        body,
        mesh=mesh,
        in_specs=(
            P("dp", None),
            P("dp"),
            P(),
            P(None, None, "tensor"),
            P(None, "tensor"),
            P("tensor", None),
            P(None, None, "tensor"),
            P("tensor", None),
            P("dp", None),
        ),
        out_specs=(
            P(("dp", "tensor"), None),
            P(("dp", "tensor"), None),
            P(),
            P(None, "dp", "tensor"),
            P(),
            P("tensor", "dp"),
            P(None, "dp", "tensor"),
            P("tensor", "dp"),
        ),
        check_vma=False,
    )
```

time: 883 us -> 483 us (0.55)
  waiting for transfers between devices: 527 us -> 165 us
  other arithmetic: 93.9 us -> 42.1 us
  blocking collectives: 39.9 us -> 0 us
  starting transfers between devices: 7.31 us -> 41.8 us
  matrix products: 153 us -> 179 us
  between operations: 15.2 us -> 3.63 us
    reduce_scatter x4 -> x0, waiting for transfers between devices: 278 us -> none  [the longest x1 96.1 us: body(): lax.psum_scatter(grad_ffn.astype(jnp.bfloat16), 'dp', scatter_dimension=1...]
    psum x2 -> x0, waiting for transfers between devices: 241 us -> none  [the longest x1 122 us: body(): lax.psum(jnp.dot(gated_mix, out_weight, preferred_element_type=jnp.float3...]
    ppermute x2 -> x40, waiting for transfers between devices: 0.36 us -> 165 us  [the longest x38 163 us: swap(): return lax.ppermute(value, axis, [(i, i ^ bits) for i in range(peers)])]
    psum x1 -> x0, blocking collectives: 39.9 us -> none  [body(): lax.psum((jnp.stack([gain_one, gain_two]), conv_full), ('dp', 'tensor'))]
    ppermute x2 -> x40, starting transfers between devices: 6.13 us -> 41.8 us  [the longest x38 36.4 us: swap(): return lax.ppermute(value, axis, [(i, i ^ bits) for i in range(peers)])]
    dot_general x12 -> x30, matrix products: 153 us -> 179 us  [matmul(): return lax.dot_general(a, b, (dims, ((), ())), preferred_element_type=F32)]
    add x4 -> x10, other arithmetic: 27.2 us -> 10.6 us  [the longest x1 6.06 us: body(): d_res + norm_backward(d_ni, x_normed, inverse_one, norm_gains[0])]
    reduce_sum x3 -> x1, other arithmetic: 13.7 us -> 1.34 us  [body(): gain_two = jnp.sum(d_nf * resid_normed, axis=0)]
  transfers between devices with their start and end apart: 10 -> 40, of which waited for: 9 -> 14; matrix products, arithmetic and copies ran while one was open for 15% -> 51% of each run, Pallas kernels for 0% -> 0%
where the time goes in v1:
time: 483 us; the launch traced here: 477 us
  matrix products  179 us (37%)
  waiting for transfers between devices  165 us (34%)
  local copies, waits for them, and re-layouts  45.6 us (9%)
  other arithmetic  42.1 us (9%)
  starting transfers between devices  41.8 us (9%)
    dot_general x30, matrix products, matmul(): return lax.dot_general(a, b, (dims, ((), ())), preferred_element_type=F32)  179 us
    ppermute x38, waiting for transfers between devices, swap(): return lax.ppermute(value, axis, [(i, i ^ bits) for i in range(peers)])  163 us
    ppermute x38, starting transfers between devices, swap(): return lax.ppermute(value, axis, [(i, i ^ bits) for i in range(peers)])  36.4 us
    unnamed x148, local copies, waits for them, and re-layouts  19.8 us
  transfers between devices with their start and end apart: 40, of which 14 were waited for; matrix products, arithmetic and copies ran while one was open for 51% of the time, Pallas kernels for 0%

profile of v1, /device:TPU:0, one launch (start us, length us, event | category | flops | bytes accessed | tf_op | source)
XLA Modules:
  0.0 476.8 jit_solution(16263519863874428760)
XLA Ops:
  19.9 19.4 %collective-permute-done.5 = f32[3,256]{1,0:T(4,128)S(1)} collective-permute-done((f32[3,256]{1,0:T(4,128)}, f32[3,256]{1,0:T(4,128)S(1)}, u32[]{:S(2)}, u32[]{:S(2)}) %collective-permute-start.5) | collective-permute-done | bytes 3104 | tf_op jit(solution)/shard_map/ppermute | solution.py:13
  80.3 9.2 %fusion.29 = f32[1536,1152]{1,0:T(8,128)} fusion(bf16[1152,1024]{1,0:T(8,128)(2,1)S(1)} %copy-done, bf16[768,1024]{1,0:T(8,128)(2,1)} %get-tuple-element.46, bf16[768,1024]{1,0:T(8,128)(2,1)} %get-tuple-element.47), kind=kOutput, calls=%fused_computation.95 | convolution fusion | flops 3630170112 | bytes 12582912 | tf_op jit(solution)/shard_map/dot_general | solution.py:82
  89.6 8.0 %fusion.27 = f32[1536,1152]{1,0:T(8,128)} fusion(bf16[1152,1024]{1,0:T(8,128)(2,1)S(1)} %copy-done, bf16[768,1024]{1,0:T(8,128)(2,1)S(1)} %copy-done.18, bf16[768,1024]{1,0:T(8,128)(2,1)S(1)} %copy-done.19), kind=kOutput, calls=%fused_computation.93 | convolution fusion | flops 3630170112 | bytes 12582912 | tf_op jit(solution)/shard_map/dot_general | solution.py:82
  99.7 9.1 %fusion.16 = f32[1536,1152]{1,0:T(8,128)} fusion(bf16[2,1024,1152]{2,1,0:T(8,128)(2,1)S(1)} %bitcast.235, bf16[768,1024]{1,0:T(8,128)(2,1)} %collective-permute-done.10, bf16[768,1024]{1,0:T(8,128)(2,1)} %multiply_convert_fusion.9), kind=kOutput, calls=%fused_computation.72 | convolution fusion | flops 3630170112 | bytes 12582912 | tf_op jit(solution)/shard_map/dot_general | solution.py:82
  108.8 13.3 %multiply_convert_fusion.2 = (bf16[1536,1152]{1,0:T(8,128)(2,1)S(1)}, bf16[1536,1152]{1,0:T(8,128)(2,1)}, bf16[1536,1152]{1,0:T(8,128)(2,1)}) fusion(f32[1536,1152]{1,0:T(8,128)} %fusion.29, f32[1536,1152]{1,0:T(8,128)} %fusion.16, bf16[2,1024,1152]{2,1,0:T(8,128)(2,1)} %param.15, bf16[768,1024]{1,0:T(8,128)(2,1)} %collective-permute-done.10, ...), kind=kOutput, calls=%fused_computation.3 | convolution fusion | flops 3656712192 | bytes 30277632 | tf_op jit(solution)/shard_map/dot_general | solution.py:82
  122.1 11.0 %fusion.20 = f32[1536,1024]{1,0:T(8,128)} fusion(bf16[1536,1152]{1,0:T(8,128)(2,1)} %get-tuple-element.37, bf16[2,1024,1152]{2,1,0:T(8,128)(2,1)} %param.15), kind=kOutput, calls=%fused_computation.76 | convolution fusion | flops 3623878656 | bytes 12189696 | tf_op jit(solution)/shard_map/dot_general | solution.py:82
  133.0 7.3 %add_convert_fusion.1 = bf16[1536,1024]{1,0:T(8,128)(2,1)S(1)} fusion(f32[1536,1024]{1,0:T(8,128)} %fusion.20, bf16[1536,1152]{1,0:T(8,128)(2,1)S(1)} %get-tuple-element.36, bf16[2,1024,1152]{2,1,0:T(8,128)(2,1)} %param.15), kind=kOutput, calls=%fused_computation.12 | convolution fusion | flops 3627024384 | bytes 15335424 | tf_op jit(solution)/shard_map/dot_general | solution.py:82
  155.4 8.5 %fusion.65 = f32[1024,1152]{1,0:T(8,128)} fusion(bf16[1536,1152]{1,0:T(8,128)(2,1)S(1)} %copy-done.52, bf16[768,1024]{1,0:T(8,128)(2,1)} %collective-permute-done.10, bf16[768,1024]{1,0:T(8,128)(2,1)} %multiply_convert_fusion.9), kind=kOutput, calls=%fused_computation.207 | convolution fusion | flops 3630170112 | bytes 11403264 | tf_op jit(solution)/shard_map/dot_general | solution.py:82
  163.9 8.4 %fusion.64 = f32[1024,1152]{1,0:T(8,128)} fusion(bf16[1536,1152]{1,0:T(8,128)(2,1)S(1)} %copy-done.51, bf16[768,1024]{1,0:T(8,128)(2,1)} %collective-permute-done.10, bf16[768,1024]{1,0:T(8,128)(2,1)} %multiply_convert_fusion.9), kind=kOutput, calls=%fused_computation.206 | convolution fusion | flops 3630170112 | bytes 11403264 | tf_op jit(solution)/shard_map/dot_general | solution.py:82
  174.1 6.2 %fusion.14 = f32[1536,1152]{1,0:T(8,128)} fusion(bf16[1536,1024]{1,0:T(8,128)(2,1)S(1)} %constant_dynamic-update-slice_fusion.12, bf16[2,1024,1152]{2,1,0:T(8,128)(2,1)S(1)} %bitcast.237), kind=kOutput, calls=%fused_computation.70 | convolution fusion | flops 3623878656 | bytes 12582912 | tf_op jit(solution)/shard_map/dot_general | solution.py:82
  180.3 14.4 %multiply_convert_fusion = (bf16[1536,1152]{1,0:T(8,128)(2,1)}, bf16[1536,1152]{1,0:T(8,128)(2,1)}, bf16[1536,1152]{1,0:T(8,128)(2,1)}) fusion(f32[1536,1152]{1,0:T(8,128)} %fusion.27, f32[1536,1152]{1,0:T(8,128)} %fusion.14, bf16[1536,1024]{1,0:T(8,128)(2,1)} %copy-done.23, bf16[2,1024,1152]{2,1,0:T(8,128)(2,1)} %param.15), kind=kOutput, calls=%fused_computation.1 | convolution fusion | flops 3650420736 | bytes 30277632 | tf_op jit(solution)/shard_map/dot_general | solution.py:82
  194.6 7.4 %add_convert_fusion.2 = bf16[1024,1152]{1,0:T(8,128)(2,1)S(1)} fusion(f32[1024,1152]{1,0:T(8,128)} %fusion.28, bf16[1536,1152]{1,0:T(8,128)(2,1)} %get-tuple-element.41, bf16[768,1024]{1,0:T(8,128)(2,1)S(1)} %copy-done.18, bf16[768,1024]{1,0:T(8,128)(2,1)S(1)} %copy-done.19), kind=kOutput, calls=%fused_computation.13 | convolution fusion | flops 3632529408 | bytes 13762560 | tf_op jit(solution)/shard_map/dot_general | solution.py:82
  204.7 7.9 %fusion.18 = f32[1536,1024]{1,0:T(8,128)} fusion(bf16[1536,1152]{1,0:T(8,128)(2,1)S(1)} %copy-done.56, bf16[2,1024,1152]{2,1,0:T(8,128)(2,1)} %param.15), kind=kOutput, calls=%fused_computation.74 | convolution fusion | flops 3623878656 | bytes 12189696 | tf_op jit(solution)/shard_map/dot_general | solution.py:82
  217.9 8.8 %add_convert_fusion = bf16[1536,1024]{1,0:T(8,128)(2,1)S(1)} fusion(f32[1536,1024]{1,0:T(8,128)} %fusion.18, bf16[1536,1152]{1,0:T(8,128)(2,1)} %get-tuple-element.39, bf16[2,1024,1152]{2,1,0:T(8,128)(2,1)} %param.15), kind=kOutput, calls=%fused_computation.11 | convolution fusion | flops 3627024384 | bytes 15335424 | tf_op jit(solution)/shard_map/dot_general | solution.py:82
  226.7 8.8 %add_convert_fusion.3 = bf16[1024,1152]{1,0:T(8,128)(2,1)S(1)} fusion(f32[1024,1152]{1,0:T(8,128)} %fusion.64, bf16[1536,1024]{1,0:T(8,128)(2,1)} %copy-done.23, bf16[1536,1152]{1,0:T(8,128)(2,1)} %get-tuple-element.39), kind=kOutput, calls=%fused_computation.14 | convolution fusion | flops 3626237952 | bytes 13762560 | tf_op jit(solution)/shard_map/dot_general | solution.py:82
  242.7 13.6 %collective-permute-done.31 = bf16[4,128,1152]{2,1,0:T(8,128)(2,1)} collective-permute-done((bf16[4,128,1152]{2,1,0:T(8,128)(2,1)S(1)}, bf16[4,128,1152]{2,1,0:T(8,128)(2,1)}, u32[]{:S(2)}, u32[]{:S(2)}) %collective-permute-start.31) | collective-permute-done | bytes 1179680 | tf_op jit(solution)/shard_map/ppermute | solution.py:13
  264.9 18.8 %collective-permute-done.34 = bf16[4,128,1152]{2,1,0:T(8,128)(2,1)S(1)} collective-permute-done((bf16[4,128,1152]{2,1,0:T(8,128)(2,1)S(1)}, bf16[4,128,1152]{2,1,0:T(8,128)(2,1)S(1)}, u32[]{:S(2)}, u32[]{:S(2)}) %collective-permute-start.34) | collective-permute-done | bytes 1179680 | tf_op jit(solution)/shard_map/ppermute | solution.py:13
  287.3 10.4 %collective-permute-done.18 = bf16[768,1024]{1,0:T(8,128)(2,1)S(1)} collective-permute-done((bf16[768,1024]{1,0:T(8,128)(2,1)S(1)}, bf16[768,1024]{1,0:T(8,128)(2,1)S(1)}, u32[]{:S(2)}, u32[]{:S(2)}) %collective-permute-start.18) | collective-permute-done | bytes 1572896 | tf_op jit(solution)/shard_map/ppermute | solution.py:13
  300.6 28.7 %collective-permute-done.15 = bf16[768,1024]{1,0:T(8,128)(2,1)S(1)} collective-permute-done((bf16[768,1024]{1,0:T(8,128)(2,1)S(1)}, bf16[768,1024]{1,0:T(8,128)(2,1)S(1)}, u32[]{:S(2)}, u32[]{:S(2)}) %collective-permute-start.15) | collective-permute-done | bytes 1572896 | tf_op jit(solution)/shard_map/ppermute | solution.py:13
  371.6 19.8 %collective-permute-done.39 = bf16[1,128,1152]{2,1,0:T(8,128)(2,1)S(1)} collective-permute-done((bf16[1,128,1152]{2,1,0:T(8,128)(2,1)S(1)}, bf16[1,128,1152]{2,1,0:T(8,128)(2,1)S(1)}, u32[]{:S(2)}, u32[]{:S(2)}) %collective-permute-start.39) | collective-permute-done | bytes 294944 | tf_op jit(solution)/shard_map/ppermute | solution.py:13
  396.2 22.9 %collective-permute-done.27 = bf16[8,4,128,256]{3,2,1,0:T(8,128)(2,1)S(1)} collective-permute-done((bf16[8,4,128,256]{3,2,1,0:T(8,128)(2,1)S(1)}, bf16[8,4,128,256]{3,2,1,0:T(8,128)(2,1)S(1)}, u32[]{:S(2)}, u32[]{:S(2)}) %collective-permute-start.27) | collective-permute-done | bytes 2097184 | tf_op jit(solution)/shard_map/ppermute | solution.py:13
  427.8 17.4 %collective-permute-done.28 = bf16[4,4,128,256]{3,2,1,0:T(8,128)(2,1)S(1)} collective-permute-done((bf16[4,4,128,256]{3,2,1,0:T(8,128)(2,1)S(1)}, bf16[4,4,128,256]{3,2,1,0:T(8,128)(2,1)S(1)}, u32[]{:S(2)}, u32[]{:S(2)}) %collective-permute-start.28) | collective-permute-done | bytes 1048608 | tf_op jit(solution)/shard_map/ppermute | solution.py:13
  453.4 6.6 %collective-permute-done.23 = f32[5,1024]{1,0:T(8,128)S(1)} collective-permute-done((f32[5,1024]{1,0:T(8,128)S(1)}, f32[5,1024]{1,0:T(8,128)S(1)}, u32[]{:S(2)}, u32[]{:S(2)}) %collective-permute-start.23) | collective-permute-done | bytes 20512 | tf_op jit(solution)/shard_map/ppermute | solution.py:13
  464.1 6.1 %multiply_add_fusion = f32[768,1024]{1,0:T(8,128)} fusion(f32[768,1024]{1,0:T(8,128)} %copy-done.10, f32[768,1024]{1,0:T(8,128)} %get-tuple-element.76, f32[784,1024]{1,0:T(8,128)} %get-tuple-element.55, f32[768]{0:T(1024)S(1)} %broadcast_multiply_fusion.3, f32[1024]{0:T(1024)S(1)} %bitcast.220, f32[768]{0:T(1024)S(1)} %copy-done.37), kind=kLoop, calls=%fused_computation.45 | loop fusion | flops 3932160 | bytes 12593152 | tf_op jit(solution)/shard_map/add | solution.py:242
  (338 shorter events, 181.4 us)
Async XLA Ops:
  0.7 46.8 %collective-permute-start.2 = (bf16[3,1024,256]{2,1,0:T(8,128)(2,1)}, bf16[3,1024,256]{2,1,0:T(8,128)(2,1)}, u32[]{:S(2)}, u32[]{:S(2)}) collective-permute-start(bf16[3,1024,256]{2,1,0:T(8,128)(2,1)} %param.12), channel_id=1, source_target_pairs={{0,2},{1,3},{2,0},{3,1},{4,6},{5,7},{6,4},{7,5},{8,10},{9,11},{10,... | collective-permute-start | bytes 4718600 | tf_op jit(solution)/shard_map/ppermute | solution.py:13
  3.7 54.2 %collective-permute-start.1 = (bf16[3,1024,256]{2,1,0:T(8,128)(2,1)}, bf16[3,1024,256]{2,1,0:T(8,128)(2,1)}, u32[]{:S(2)}, u32[]{:S(2)}) collective-permute-start(bf16[3,1024,256]{2,1,0:T(8,128)(2,1)} %param.12), channel_id=1, source_target_pairs={{0,1},{1,0},{2,3},{3,2},{4,5},{5,4},{6,7},{7,6},{8,9},{9,8},{10,11... | collective-permute-start | bytes 4718600 | tf_op jit(solution)/shard_map/ppermute | solution.py:13
  3.7 35.5 %collective-permute-start.5 = (f32[3,256]{1,0:T(4,128)}, f32[3,256]{1,0:T(4,128)S(1)}, u32[]{:S(2)}, u32[]{:S(2)}) collective-permute-start(f32[3,256]{1,0:T(4,128)} %param.13), channel_id=1, source_target_pairs={{0,2},{1,3},{2,0},{3,1},{4,6},{5,7},{6,4},{7,5},{8,10},{9,11},{10,... | collective-permute-start | bytes 9224 | tf_op jit(solution)/shard_map/ppermute | solution.py:13
  3.9 35.4 %collective-permute-start.4 = (f32[3,256]{1,0:T(4,128)}, f32[3,256]{1,0:T(4,128)S(1)}, u32[]{:S(2)}, u32[]{:S(2)}) collective-permute-start(f32[3,256]{1,0:T(4,128)} %param.13), channel_id=1, source_target_pairs={{0,1},{1,0},{2,3},{3,2},{4,5},{5,4},{6,7},{7,6},{8,9},{9,8},{10,11... | collective-permute-start | bytes 9224 | tf_op jit(solution)/shard_map/ppermute | solution.py:13
  4.2 49.0 %collective-permute-start.8 = (bf16[256,1024]{1,0:T(8,128)(2,1)}, bf16[256,1024]{1,0:T(8,128)(2,1)S(1)}, u32[]{:S(2)}, u32[]{:S(2)}) collective-permute-start(bf16[256,1024]{1,0:T(8,128)(2,1)} %param.14), channel_id=1, source_target_pairs={{0,2},{1,3},{2,0},{3,1},{4,6},{5,7},{6,4},{7,5},{8,10},{9,11},{10,... | collective-permute-start | bytes 1572872 | tf_op jit(solution)/shard_map/ppermute | solution.py:13
  98.2 56.6 %collective-permute-start.12 = (bf16[768,1024]{1,0:T(8,128)(2,1)}, bf16[768,1024]{1,0:T(8,128)(2,1)S(1)}, u32[]{:S(2)}, u32[]{:S(2)}) collective-permute-start(bf16[768,1024]{1,0:T(8,128)(2,1)} %multiply_convert_fusion.9), channel_id=1, source_target_pairs={{0,2},{1,3},{2,0},{3,1},{4,6},{5,7},{6,4},{7,5},{8,10},{9,11},{10,... | collective-permute-start | bytes 4718600 | tf_op jit(solution)/shard_map/ppermute | solution.py:13
  141.7 145.6 %collective-permute-start.16 = (bf16[768,1024]{1,0:T(8,128)(2,1)}, bf16[768,1024]{1,0:T(8,128)(2,1)S(1)}, u32[]{:S(2)}, u32[]{:S(2)}) collective-permute-start(bf16[768,1024]{1,0:T(8,128)(2,1)} %slice.277), channel_id=1, source_target_pairs={{0,1},{1,0},{2,3},{3,2},{4,5},{5,4},{6,7},{7,6},{8,9},{9,8},{10,11... | collective-permute-start | bytes 4718600 | tf_op jit(solution)/shard_map/ppermute | solution.py:13
  147.7 153.0 %collective-permute-start.11 = (bf16[768,1024]{1,0:T(8,128)(2,1)}, bf16[768,1024]{1,0:T(8,128)(2,1)}, u32[]{:S(2)}, u32[]{:S(2)}) collective-permute-start(bf16[768,1024]{1,0:T(8,128)(2,1)} %slice.273), channel_id=1, source_target_pairs={{0,1},{1,0},{2,3},{3,2},{4,5},{5,4},{6,7},{7,6},{8,9},{9,8},{10,11... | collective-permute-start | bytes 4718600 | tf_op jit(solution)/shard_map/ppermute | solution.py:13
  202.2 38.4 %collective-permute-start.37 = (bf16[4,128,1152]{2,1,0:T(8,128)(2,1)S(1)}, bf16[4,128,1152]{2,1,0:T(8,128)(2,1)}, u32[]{:S(2)}, u32[]{:S(2)}) collective-permute-start(bf16[4,128,1152]{2,1,0:T(8,128)(2,1)S(1)} %dynamic-slice_bitcast_fusion), channel_id=1, source_target_pairs={{0,4},{4,0},{8,12},{12,8},{16,20},{20,16},{24,28},{28,24},{1,5},{5... | collective-permute-start | bytes 3538952 | tf_op jit(solution)/shard_map/ppermute | solution.py:13
  217.8 38.5 %collective-permute-start.31 = (bf16[4,128,1152]{2,1,0:T(8,128)(2,1)S(1)}, bf16[4,128,1152]{2,1,0:T(8,128)(2,1)}, u32[]{:S(2)}, u32[]{:S(2)}) collective-permute-start(bf16[4,128,1152]{2,1,0:T(8,128)(2,1)S(1)} %dynamic-slice_bitcast_fusion.2), channel_id=1, source_target_pairs={{0,4},{4,0},{8,12},{12,8},{16,20},{20,16},{24,28},{28,24},{1,5},{5... | collective-permute-start | bytes 3538952 | tf_op jit(solution)/shard_map/ppermute | solution.py:13
  235.6 23.9 %collective-permute-start.17 = (bf16[768,1024]{1,0:T(8,128)(2,1)S(1)}, bf16[768,1024]{1,0:T(8,128)(2,1)S(1)}, u32[]{:S(2)}, u32[]{:S(2)}) collective-permute-start(bf16[768,1024]{1,0:T(8,128)(2,1)S(1)} %slice.279), channel_id=1, source_target_pairs={{0,1},{1,0},{2,3},{3,2},{4,5},{5,4},{6,7},{7,6},{8,9},{9,8},{10,11... | collective-permute-start | bytes 4718600 | tf_op jit(solution)/shard_map/ppermute | solution.py:13
  240.6 21.2 %collective-permute-start.14 = (bf16[768,1024]{1,0:T(8,128)(2,1)S(1)}, bf16[768,1024]{1,0:T(8,128)(2,1)S(1)}, u32[]{:S(2)}, u32[]{:S(2)}) collective-permute-start(bf16[768,1024]{1,0:T(8,128)(2,1)S(1)} %slice.275), channel_id=1, source_target_pairs={{0,1},{1,0},{2,3},{3,2},{4,5},{5,4},{6,7},{7,6},{8,9},{9,8},{10,11... | collective-permute-start | bytes 4718600 | tf_op jit(solution)/shard_map/ppermute | solution.py:13
  256.3 27.4 %collective-permute-start.34 = (bf16[4,128,1152]{2,1,0:T(8,128)(2,1)S(1)}, bf16[4,128,1152]{2,1,0:T(8,128)(2,1)S(1)}, u32[]{:S(2)}, u32[]{:S(2)}) collective-permute-start(bf16[4,128,1152]{2,1,0:T(8,128)(2,1)S(1)} %dynamic-slice_bitcast_fusion.1), channel_id=1, source_target_pairs={{0,4},{4,0},{8,12},{12,8},{16,20},{20,16},{24,28},{28,24},{1,5},{5... | collective-permute-start | bytes 3538952 | tf_op jit(solution)/shard_map/ppermute | solution.py:13
  260.3 37.4 %collective-permute-start.18 = (bf16[768,1024]{1,0:T(8,128)(2,1)S(1)}, bf16[768,1024]{1,0:T(8,128)(2,1)S(1)}, u32[]{:S(2)}, u32[]{:S(2)}) collective-permute-start(bf16[768,1024]{1,0:T(8,128)(2,1)S(1)} %add_convert_fusion.6), channel_id=1, source_target_pairs={{0,2},{1,3},{2,0},{3,1},{4,6},{5,7},{6,4},{7,5},{8,10},{9,11},{10,... | collective-permute-start | bytes 4718600 | tf_op jit(solution)/shard_map/ppermute | solution.py:13
  262.5 66.8 %collective-permute-start.15 = (bf16[768,1024]{1,0:T(8,128)(2,1)S(1)}, bf16[768,1024]{1,0:T(8,128)(2,1)S(1)}, u32[]{:S(2)}, u32[]{:S(2)}) collective-permute-start(bf16[768,1024]{1,0:T(8,128)(2,1)S(1)} %add_convert_fusion.9), channel_id=1, source_target_pairs={{0,2},{1,3},{2,0},{3,1},{4,6},{5,7},{6,4},{7,5},{8,10},{9,11},{10,... | collective-permute-start | bytes 4718600 | tf_op jit(solution)/shard_map/ppermute | solution.py:13
  283.7 76.7 %collective-permute-start.38 = (bf16[2,128,1152]{2,1,0:T(8,128)(2,1)}, bf16[2,128,1152]{2,1,0:T(8,128)(2,1)}, u32[]{:S(2)}, u32[]{:S(2)}) collective-permute-start(bf16[2,128,1152]{2,1,0:T(8,128)(2,1)} %dynamic-slice_bitcast_fusion.4), channel_id=1, source_target_pairs={{0,8},{4,12},{8,0},{12,4},{16,24},{20,28},{24,16},{28,20},{1,9},{5... | collective-permute-start | bytes 1769480 | tf_op jit(solution)/shard_map/ppermute | solution.py:13
  287.3 77.1 %collective-permute-start.32 = (bf16[2,128,1152]{2,1,0:T(8,128)(2,1)}, bf16[2,128,1152]{2,1,0:T(8,128)(2,1)}, u32[]{:S(2)}, u32[]{:S(2)}) collective-permute-start(bf16[2,128,1152]{2,1,0:T(8,128)(2,1)} %dynamic-slice_bitcast_fusion.6), channel_id=1, source_target_pairs={{0,8},{4,12},{8,0},{12,4},{16,24},{20,28},{24,16},{28,20},{1,9},{5... | collective-permute-start | bytes 1769480 | tf_op jit(solution)/shard_map/ppermute | solution.py:13
  297.7 68.3 %collective-permute-start.35 = (bf16[2,128,1152]{2,1,0:T(8,128)(2,1)}, bf16[2,128,1152]{2,1,0:T(8,128)(2,1)}, u32[]{:S(2)}, u32[]{:S(2)}) collective-permute-start(bf16[2,128,1152]{2,1,0:T(8,128)(2,1)} %dynamic-slice_bitcast_fusion.5), channel_id=1, source_target_pairs={{0,8},{4,12},{8,0},{12,4},{16,24},{20,28},{24,16},{28,20},{1,9},{5... | collective-permute-start | bytes 1769480 | tf_op jit(solution)/shard_map/ppermute | solution.py:13
  361.7 29.8 %collective-permute-start.39 = (bf16[1,128,1152]{2,1,0:T(8,128)(2,1)S(1)}, bf16[1,128,1152]{2,1,0:T(8,128)(2,1)S(1)}, u32[]{:S(2)}, u32[]{:S(2)}) collective-permute-start(bf16[1,128,1152]{2,1,0:T(8,128)(2,1)S(1)} %constant_dynamic-slice_fusion), channel_id=1, source_target_pairs={{0,16},{4,20},{8,24},{12,28},{16,0},{20,4},{24,8},{28,12},{1,17},{... | collective-permute-start | bytes 884744 | tf_op jit(solution)/shard_map/ppermute | solution.py:13
  365.6 60.4 %collective-permute-start.33 = (bf16[1,128,1152]{2,1,0:T(8,128)(2,1)S(1)}, bf16[1,128,1152]{2,1,0:T(8,128)(2,1)S(1)}, u32[]{:S(2)}, u32[]{:S(2)}) collective-permute-start(bf16[1,128,1152]{2,1,0:T(8,128)(2,1)S(1)} %constant_dynamic-slice_fusion.2), channel_id=1, source_target_pairs={{0,16},{4,20},{8,24},{12,28},{16,0},{20,4},{24,8},{28,12},{1,17},{... | collective-permute-start | bytes 884744 | tf_op jit(solution)/shard_map/ppermute | solution.py:13
  367.4 80.6 %collective-permute-start.36 = (bf16[1,128,1152]{2,1,0:T(8,128)(2,1)S(1)}, bf16[1,128,1152]{2,1,0:T(8,128)(2,1)S(1)}, u32[]{:S(2)}, u32[]{:S(2)}) collective-permute-start(bf16[1,128,1152]{2,1,0:T(8,128)(2,1)S(1)} %constant_dynamic-slice_fusion.1), channel_id=1, source_target_pairs={{0,16},{4,20},{8,24},{12,28},{16,0},{20,4},{24,8},{28,12},{1,17},{... | collective-permute-start | bytes 884744 | tf_op jit(solution)/shard_map/ppermute | solution.py:13
  370.2 26.0 %collective-permute-start.25 = (bf16[8,4,128,256]{3,2,1,0:T(8,128)(2,1)S(1)}, bf16[8,4,128,256]{3,2,1,0:T(8,128)(2,1)S(1)}, u32[]{:S(2)}, u32[]{:S(2)}) collective-permute-start(bf16[8,4,128,256]{3,2,1,0:T(8,128)(2,1)S(1)} %bitcast.213), channel_id=1, source_target_pairs={{0,1},{1,0},{2,3},{3,2},{4,5},{5,4},{6,7},{7,6},{8,9},{9,8},{10,11... | collective-permute-start | bytes 6291464 | tf_op jit(solution)/shard_map/ppermute | solution.py:13
  371.1 48.1 %collective-permute-start.27 = (bf16[8,4,128,256]{3,2,1,0:T(8,128)(2,1)S(1)}, bf16[8,4,128,256]{3,2,1,0:T(8,128)(2,1)S(1)}, u32[]{:S(2)}, u32[]{:S(2)}) collective-permute-start(bf16[8,4,128,256]{3,2,1,0:T(8,128)(2,1)S(1)} %fusion.2), channel_id=1, source_target_pairs={{0,2},{1,3},{2,0},{3,1},{4,6},{5,7},{6,4},{7,5},{8,10},{9,11},{10,... | collective-permute-start | bytes 6291464 | tf_op jit(solution)/shard_map/ppermute | solution.py:13
  420.4 24.8 %collective-permute-start.28 = (bf16[4,4,128,256]{3,2,1,0:T(8,128)(2,1)S(1)}, bf16[4,4,128,256]{3,2,1,0:T(8,128)(2,1)S(1)}, u32[]{:S(2)}, u32[]{:S(2)}) collective-permute-start(bf16[4,4,128,256]{3,2,1,0:T(8,128)(2,1)S(1)} %dynamic-slice_bitcast_fusion.3), channel_id=1, source_target_pairs={{0,4},{4,0},{8,12},{12,8},{16,20},{20,16},{24,28},{28,24},{1,5},{5... | collective-permute-start | bytes 3145736 | tf_op jit(solution)/shard_map/ppermute | solution.py:13
  (85 other events, 1039.5 us)
